TPU v7x, 32 devices: a whole 2x2x4 slice. The times are simulated.
32 devices in a mesh: rows: 8 (over y, x, core), rep: 4 (over z).
Axes of the slice: x: 2, y: 2, z: 4, core: 2. Of those that a mesh axis runs over, the one named last changes fastest.
Arguments:
- features: float32 [4096, 256], P(('rows', 'rep')), may hold values from -6 to 6
- weight: float32 [256, 256], replicated, may hold values from -0.375 to 0.375
- cotangent: float32 [4096, 256], P(('rows', 'rep')), may hold values from -6 to 6
- tiles: float32 [8, 4, 8, 2, 128, 128], P('rows', 'rep'), may hold values from -0.125 to 0.125
- tile_count: int32 [8, 4, 8], P('rows', 'rep'), may hold values from 0 to 2, as said below
- tile_block: int32 [8, 4, 8, 2], P('rows', 'rep'), may hold values from 0 to 3, as said below
Outputs:
- hidden: float32 [4096, 256], P(('rows', 'rep'))
- grad_weight: float32 [256, 256], replicated
- grad_features: float32 [4096, 256], P(('rows', 'rep'))
Inputs may be any that keep to these rules, and one draw needn't show every extreme that they name: `tile_count`: at the section equal to the row group, every column block holds 2 live tiles. `tile_block`: the blocks named by one section's slots are distinct; slots at or beyond the section's count are ignored.
All inputs are finite; a program needn't handle non-finite values.
Results may differ from a plain program's by a relative error of at most 0.0001.
Values sent between devices are 32-bit elements; how exact they have to be, the bound alone decides.
A program may use at most 128 MiB of HBM per device.

v0:
```python
import math

import jax
import jax.numpy as jnp
from jax import lax
from jax.sharding import PartitionSpec as P


def silu_slope(pre):
    sig = jax.nn.sigmoid(pre)
    return sig * (1.0 + pre * (1.0 - sig))


def body(features, weight, cotangent, tiles, tile_count, tile_block):
    highest = lax.Precision.HIGHEST
    tile_set = tiles[0, 0]
    counts = tile_count[0, 0]
    block_ids = tile_block[0, 0]
    sections = tile_set.shape[0]
    slots = tile_set.shape[1]
    blk = tile_set.shape[2]
    width = features.shape[1]
    groups = lax.axis_size("rep")
    select = (
        (block_ids[..., None] == jnp.arange(groups, dtype=jnp.int32))
        & (jnp.arange(slots, dtype=jnp.int32)[:, None] < counts[:, None, None])
    ).astype(jnp.float32)
    gathered = lax.all_gather(features, "rows", axis=0, tiled=True).reshape(sections, blk, width)
    prods = jnp.einsum("stab,sbf->staf", tile_set, gathered, precision=highest)
    total = jnp.einsum("stk,staf->kaf", select, prods, precision=highest)
    aggregated = lax.psum_scatter(
        total.reshape(groups * blk, width), "rep", scatter_dimension=0, tiled=True
    )
    pre = jnp.dot(aggregated, weight, precision=highest)
    hidden = jax.nn.silu(pre)
    delta = cotangent * silu_slope(pre)
    weight_term = jnp.dot(aggregated.T, delta, precision=highest)
    node_total = blk * lax.axis_size("rows") * groups
    grad_weight = lax.psum(weight_term, ("rows", "rep")) / math.sqrt(node_total)
    back = jnp.dot(delta, weight.T, precision=highest)
    group_back = lax.all_gather(back, "rep", axis=0, tiled=True).reshape(groups, blk, width)
    count = sections * blk
    picked = jnp.einsum("stk,kaf->staf", select, group_back, precision=highest)
    result = jnp.einsum("stab,staf->sbf", tile_set, picked, precision=highest)
    all_terms = result.reshape(count, width)
    grad_features = lax.psum_scatter(all_terms, "rows", scatter_dimension=0, tiled=True)
    return (hidden, grad_weight, grad_features)


def solution(mesh):
    in_specs = (
        P(("rows", "rep"), None),
        P(),
        P(("rows", "rep"), None),
        P("rows", "rep", None, None, None, None),
        P("rows", "rep", None),
        P("rows", "rep", None, None),
    )
    out_specs = (P(("rows", "rep"), None), P(), P(("rows", "rep"), None))
    return jax.shard_map(body, mesh=mesh, in_specs=in_specs, out_specs=out_specs, check_vma=False)
```

profile of v0, /device:TPU:0, one launch (start us, length us, event | category | flops | bytes accessed | tf_op | source)
XLA Modules:
  0.0 238.8 jit_solution(10158383478714156520)
XLA Ops:
  7.2 0.0 copy-start
  7.2 0.0 all-gather.2.cloned.1.call-start
  7.2 0.7 all-gather.2.cloned.1.call-update
  7.9 0.0 reduce-scatter.3.cloned.1.call-start
  8.0 0.7 iota_compare_fusion.1
  8.6 27.5 %all-gather.2.cloned.1.call-done = f32[1024,256]{1,0:T(8,128)} async-done(((f32[128,256]{1,0:T(8,128)}), f32[1024,256]{1,0:T(8,128)}) %all-gather.2.cloned.1.call-update) | async-done | bytes 1048592 | tf_op jit(solution)/shard_map/all_gather | solution.py:28
  36.1 0.0 copy-done
  36.1 0.0 copy-start.2
  36.1 3.1 %fusion.8 = f32[8,2,128,256]{3,2,1,0:T(8,128)S(1)} fusion(f32[8,128,256,1]{2,1,3,0:T(8,128)} %bitcast.40, f32[1,1,8,2,128,128]{5,4,3,2,1,0:T(8,128)S(1)} %copy-done), kind=kOutput, calls=%fused_computation.6 | convolution fusion | flops 805306368 | bytes 4194304 | tf_op jit(solution)/shard_map/stab,sbf->staf/dot_general | solution.py:29
  39.2 0.0 copy-done.2
  39.2 0.0 copy-start.1
  39.2 0.0 copy-start.3
  39.2 2.1 fusion.4
  41.3 0.9 copy.10
  42.2 0.0 reduce-scatter.3.cloned.1.call-update
  42.2 0.0 all-reduce.2.cloned.1.call-start
  42.3 21.7 %reduce-scatter.3.cloned.1.call-done = f32[128,256]{1,0:T(8,128)} async-done(((f32[512,256]{1,0:T(8,128)}), f32[128,256]{1,0:T(8,128)}) %reduce-scatter.3.cloned.1.call-update) | async-done | bytes 131088 | tf_op jit(solution)/shard_map/reduce_scatter | solution.py:31
  64.0 0.0 copy-done.1
  64.0 1.9 fusion.12
  65.9 0.0 copy-done.3
  65.9 0.4 fusion.22
  66.3 2.0 fusion.23
  68.3 0.0 all-reduce.2.cloned.1.call-update
  68.3 0.0 reduce-scatter.5.cloned.1.call-start
  68.4 15.9 %all_gather.7 = f32[512,256]{1,0:T(8,128)S(1)} all-gather(f32[128,256]{1,0:T(8,128)S(1)} %fusion.22), channel_id=1, replica_groups=mesh['rows'=8,'rep'=4] {'rep'}, dimensions={0}, use_global_device_ids=true | all-gather | bytes 655360 | tf_op jit(solution)/shard_map/all_gather | solution.py:41
  84.3 1.3 fusion.10
  85.5 3.6 %fusion = f32[8,256,128,1]{1,2,3,0:T(8,128)} fusion(f32[8,2,128,256]{3,0,2,1:T(8,128)S(1)} %fusion.10, f32[1,1,8,2,128,128]{5,4,3,2,1,0:T(8,128)S(1)} %copy-done), kind=kOutput, calls=%fused_computation | convolution fusion | flops 805306368 | bytes 4194304 | tf_op jit(solution)/shard_map/stab,staf->sbf/dot_general | solution.py:44
  89.1 0.0 reduce-scatter.5.cloned.1.call-update
  89.2 104.4 %all-reduce.2.cloned.1.call-done = f32[256,256]{1,0:T(8,128)} async-done(((f32[256,256]{1,0:T(8,128)}), f32[256,256]{1,0:T(8,128)}) %all-reduce.2.cloned.1.call-update) | async-done | bytes 262160 | tf_op jit(solution)/shard_map/psum | solution.py:39
  193.5 1.7 broadcast_multiply_fusion
  195.2 37.0 %reduce-scatter.5.cloned.1.call-done = f32[128,256]{1,0:T(8,128)} async-done(((f32[1024,256]{1,0:T(8,128)}), f32[128,256]{1,0:T(8,128)}) %reduce-scatter.5.cloned.1.call-update) | async-done | bytes 131088 | tf_op jit(solution)/shard_map/reduce_scatter | solution.py:46
Async XLA Ops:
  7.2 29.0 %copy-start = (f32[1,1,8,2,128,128]{5,4,3,2,1,0:T(8,128)S(1)}, f32[1,1,8,2,128,128]{5,4,3,2,1,0:T(8,128)}, u32[]{:S(2)}) copy-start(f32[1,1,8,2,128,128]{5,4,3,2,1,0:T(8,128)} %param.9) | copy-start | bytes 3145732
  7.2 28.9 %all-gather.2.cloned.1.call-start = ((), (), s32[]{:S(2)}) async-start(), calls=%async_computation.2 | async-start | bytes 1179648 | tf_op jit(solution)/shard_map/all_gather | solution.py:28
  7.9 56.1 %reduce-scatter.3.cloned.1.call-start = ((), (), s32[]{:S(2)}) async-start(), calls=%async_computation.3 | async-start | bytes 655360 | tf_op jit(solution)/shard_map/reduce_scatter | solution.py:31
  36.1 3.1 %copy-start.2 = (s32[1,1,8,2]{2,3,1,0:T(2,128)S(1)}, s32[1,1,8,2]{2,3,1,0:T(2,128)}, u32[]{:S(2)}) copy-start(s32[1,1,8,2]{2,3,1,0:T(2,128)} %param.11) | copy-start | bytes 196
  39.2 24.8 %copy-start.1 = (f32[256,256]{1,0:T(8,128)S(1)}, f32[256,256]{1,0:T(8,128)}, u32[]{:S(2)}) copy-start(f32[256,256]{1,0:T(8,128)} %param.7) | copy-start | bytes 786436
  39.2 26.7 %copy-start.3 = (f32[128,256]{1,0:T(8,128)S(1)}, f32[128,256]{1,0:T(8,128)}, u32[]{:S(2)}) copy-start(f32[128,256]{1,0:T(8,128)} %param.8) | copy-start | bytes 393220
  42.2 151.3 %all-reduce.2.cloned.1.call-start = ((), (), s32[]{:S(2)}) async-start(), calls=%async_computation.4 | async-start | bytes 524288 | tf_op jit(solution)/shard_map/psum | solution.py:39
  68.3 163.9 %reduce-scatter.5.cloned.1.call-start = ((), (), s32[]{:S(2)}) async-start(), calls=%async_computation.5 | async-start | bytes 1179648 | tf_op jit(solution)/shard_map/reduce_scatter | solution.py:46
Sparse Core Ops, SparseCore 0:
  9.9 26.1 all-gather.1
  42.4 21.6 reduce-scatter.2
  70.1 123.3 all-reduce.1
  197.1 35.0 reduce-scatter.4
where the time goes:
time: 239 us
  waiting for transfers between devices  191 us (80%)
  blocking collectives  15.9 us (7%)
  matrix products  14.3 us (6%)
  between operations  13.8 us (6%)
    psum x1, waiting for transfers between devices, body(): grad_weight = lax.psum(weight_term, ('rows', 'rep')) / math.sqrt(node_total)  104 us
    reduce_scatter x1, waiting for transfers between devices, body(): lax.psum_scatter(all_terms, 'rows', scatter_dimension=0, tiled=True)  37 us
    all_gather x1, waiting for transfers between devices, body(): lax.all_gather(features, 'rows', axis=0, tiled=True)  27.5 us
    reduce_scatter x1, waiting for transfers between devices, body(): lax.psum_scatter(total.reshape(groups * blk, width), 'rep', scatter_dimen...  21.7 us
    all_gather x1, blocking collectives, body(): lax.all_gather(back, 'rep', axis=0, tiled=True).reshape(groups, blk, width)  15.9 us
  transfers between devices with their start and end apart: 4, of which 4 were waited for; matrix products, arithmetic and copies ran while one was open for 3% of the time, Pallas kernels for 0%

commit v1 on v0

--- a/solution.py
+++ b/solution.py
@@ -1,9 +1,277 @@
+import functools
 import math
 
 import jax
 import jax.numpy as jnp
 from jax import lax
+from jax.experimental import pallas as pl
+from jax.experimental.pallas import tpu as pltpu
 from jax.sharding import PartitionSpec as P
+
+MESH = pl.DeviceIdType.MESH
+F32 = jnp.float32
+BF16 = jnp.bfloat16
+
+
+def split(x):
+    hi = x.astype(BF16)
+    return hi, (x - hi.astype(F32)).astype(BF16)
+
+
+def mm(a, b, dims=((1,), (0,))):
+    return lax.dot_general(a, b, (dims, ((), ())), preferred_element_type=F32)
+
+
+def mm3(a, b, dims=((1,), (0,))):
+    (ah, al), (bh, bl) = split(a), split(b)
+    return mm(ah, bh, dims) + (mm(ah, bl, dims) + mm(al, bh, dims))
+
+
+def kernel(feat, weight, cot, tiles, cnt, blks, hid_o, gw_o, gf_o,
+           G, T, W, C, Ahi, Alo, AThi, ATlo, Pb, Rb, Bk, Rs, Es, Ec, Er, Ho, Fo,
+           wt, ws, wc, wr, wz, wzr, gw,
+           loc_sem, a_s, a_r, b_s, b_r, d_s, d_r, e_s, e_r, g_s, g_r):
+    blk = T.shape[2]
+    secs = T.shape[0]
+    reps = Pb.shape[1]
+    chips = secs // 2
+    quarter = reps * blk
+    row = lax.axis_index("rows")
+    z = lax.axis_index("rep")
+    c = row % 2
+    q = row // 2
+    x = q % 2
+    y = q // 2
+    sib = row + 1 - 2 * c
+    xn = row + 2 - 4 * x
+    yn = row + 4 - 8 * y
+    dg = xn + yn - row
+    plane = (xn, yn, dg)
+    zs = [(z + d) % reps for d in range(1, reps)]
+
+    barrier = pltpu.get_barrier_semaphore()
+    peers = [(sib, z)] + [(p, z) for p in plane] + [(row, k) for k in zs]
+    for dev in peers:
+        pl.semaphore_signal(barrier, inc=1, device_id=dev, device_id_type=MESH)
+    loads = [pltpu.make_async_copy(feat.at[:, h * blk:(h + 1) * blk], G.at[h, row], loc_sem.at[h]) for h in range(2)]
+    loads += [pltpu.make_async_copy(tiles.at[0, 0], T, loc_sem.at[2]),
+              pltpu.make_async_copy(weight, W, loc_sem.at[3]),
+              pltpu.make_async_copy(cot, C, loc_sem.at[4])]
+    for ld in loads:
+        ld.start()
+    pl.semaphore_wait(barrier, len(peers))
+
+    sent = []
+
+    def send(src, dst, ss, rs, dev):
+        cp = pltpu.make_async_remote_copy(src_ref=src, dst_ref=dst, send_sem=ss, recv_sem=rs,
+                                          device_id=dev, device_id_type=MESH)
+        cp.start()
+        sent.append(cp)
+        return cp
+
+    a_cp = []
+    for h in range(2):
+        loads[h].wait()
+        mine = G.at[h, row]
+        a_cp.append([send(mine, mine, a_s.at[h, i], a_r.at[h, i], (p, z)) for i, p in enumerate((xn, yn, dg, sib))])
+
+    loads[2].wait()
+
+    def masks(s, k):
+        n = cnt[0, 0, s]
+        return [jnp.where((blks[0, 0, s, t] == k) & (t < n), 1.0, 0.0).astype(F32) for t in range(T.shape[1])]
+
+    @pl.loop(0, secs)
+    def _(s):
+        for k in range(reps):
+            m = masks(s, k)
+            val = T[s, 0] * m[0]
+            for t in range(1, T.shape[1]):
+                val = val + T[s, t] * m[t]
+            hi, lo = split(val)
+            cols = pl.ds(pl.multiple_of(s * blk, blk), blk)
+            Ahi[k * blk:(k + 1) * blk, cols] = hi
+            Alo[k * blk:(k + 1) * blk, cols] = lo
+
+    b_cp = []
+    for h in range(2):
+        fwd = []
+        for i, p in enumerate(plane):
+            a_cp[h][i].wait_recv()
+            fwd.append(send(G.at[h, p], G.at[h, p], a_s.at[h, 4 + i], a_r.at[h, 4 + i], (sib, z)))
+        a_cp[h][3].wait_recv()
+        for cp in fwd:
+            cp.wait_recv()
+        fh, fl = split(G[h].reshape(secs * blk, blk))
+        rhs = jnp.concatenate([fh, fl], axis=1)
+        acc = mm(Ahi[...], rhs)
+        acc = acc[:, :blk] + (acc[:, blk:] + mm(Alo[...], fh))
+        Pb[h] = acc.reshape(reps, blk, blk)
+        b_cp.append([send(Pb.at[h, k], Rb.at[h, i], b_s.at[h, i], b_r.at[h, i], (row, k)) for i, k in enumerate(zs)])
+
+    @pl.loop(0, secs)
+    def _(s):
+        tt = [T[s, t].T for t in range(T.shape[1])]
+        rows = pl.ds(pl.multiple_of(((s % 2) * chips + s // 2) * blk, blk), blk)
+        for k in range(reps):
+            m = masks(s, k)
+            val = tt[0] * m[0]
+            for t in range(1, T.shape[1]):
+                val = val + tt[t] * m[t]
+            hi, lo = split(val)
+            AThi[rows, k * blk:(k + 1) * blk] = hi
+            ATlo[rows, k * blk:(k + 1) * blk] = lo
+
+    loads[3].wait()
+    loads[4].wait()
+    agg = []
+    for h in range(2):
+        part = Pb[h, z]
+        for i in range(reps - 1):
+            b_cp[h][i].wait_recv()
+            part = part + Rb[h, i]
+        agg.append(part)
+    agg = jnp.concatenate(agg, axis=1)
+    w = W[...]
+    pre = mm3(agg, w)
+    sig = 1.0 / (1.0 + jnp.exp(-pre))
+    delta = C[...] * (sig * (1.0 + pre * (1.0 - sig)))
+    back = mm3(delta, w, ((1,), (1,)))
+    d_cp = []
+    for h in range(2):
+        Bk[h, z] = back[:, h * blk:(h + 1) * blk]
+        mine = Bk.at[h, z]
+        d_cp.append([send(mine, mine, d_s.at[h, i], d_r.at[h, i], (row, k)) for i, k in enumerate(zs)])
+    Ho[...] = pre * sig
+    hid_cp = pltpu.make_async_copy(Ho, hid_o, loc_sem.at[5])
+    hid_cp.start()
+
+    wt[...] = mm3(agg.T, delta) * (1.0 / math.sqrt(blk * secs * reps))
+    half = wt.shape[0] // 2
+    piece = half // chips
+    sub = piece // reps
+    oth = pl.multiple_of((1 - c) * half, half)
+    own = pl.multiple_of(c * half, half)
+    g1 = send(wt.at[pl.ds(oth, half)], ws, g_s.at[0], g_r.at[0], (sib, z))
+    g1.wait_recv()
+    wc[...] = wt[pl.ds(own, half)] + ws[...]
+    g2 = [send(wc.at[pl.ds(pl.multiple_of((p // 2) * piece, piece), piece)], wr.at[i], g_s.at[1 + i], g_r.at[1 + i], (p, z))
+          for i, p in enumerate(plane)]
+
+    def rows_start(h):
+        for cp in d_cp[h]:
+            cp.wait_recv()
+        bh, bl = split(Bk[h].reshape(quarter, blk))
+        rhs = jnp.concatenate([bh, bl], axis=1)
+        out = None
+        for first, core in ((True, 1 - c), (False, c)):
+            at = pl.ds(pl.multiple_of(core * (chips * blk), chips * blk), chips * blk)
+            acc = mm(AThi[at], rhs)
+            acc = acc[:, :blk] + (acc[:, blk:] + mm(ATlo[at], bh))
+            Rs[h, 0 if first else 1] = acc.reshape(chips, blk, blk)
+            if first:
+                out = send(Rs.at[h, 0], Es.at[h], e_s.at[h, 0], e_r.at[h, 0], (sib, z))
+        return out
+
+    def rows_mid(h, cp):
+        cp.wait_recv()
+        out = []
+        for i, p in enumerate((dg, xn, yn)):
+            Ec[h, i] = Rs[h, 1, p // 2] + Es[h, p // 2]
+            out.append(send(Ec.at[h, i], Er.at[h, i], e_s.at[h, 1 + i], e_r.at[h, 1 + i], (p, z)))
+        return out
+
+    def rows_end(h, cps):
+        total = Rs[h, 1, q] + Es[h, q]
+        for i, cp in enumerate(cps):
+            cp.wait_recv()
+            total = total + Er[h, i]
+        Fo[:, h * blk:(h + 1) * blk] = total
+
+    e0 = rows_start(0)
+    e0 = rows_mid(0, e0)
+
+    at = pl.multiple_of(q * piece, piece)
+    total = wc[pl.ds(at, piece)]
+    for i in range(3):
+        g2[i].wait_recv()
+        total = total + wr[i]
+    wz[...] = total
+    g3 = [send(wz.at[pl.ds(pl.multiple_of(k * sub, sub), sub)], wzr.at[i], g_s.at[4 + i], g_r.at[4 + i], (row, k))
+          for i, k in enumerate(zs)]
+
+    e1 = rows_start(1)
+    e1 = rows_mid(1, e1)
+
+    total = wz[pl.ds(pl.multiple_of(z * sub, sub), sub)]
+    for i in range(reps - 1):
+        g3[i].wait_recv()
+        total = total + wzr[i]
+    top = c * half + q * piece
+    mine = pl.ds(pl.multiple_of(top + z * sub, sub), sub)
+    gw[mine] = total
+    g4 = [send(gw.at[mine], gw.at[mine], g_s.at[7 + i], g_r.at[7 + i], (row, k)) for i, k in enumerate(zs)]
+    for cp in g4:
+        cp.wait_recv()
+    mine = pl.ds(pl.multiple_of(top, piece), piece)
+    g5 = [send(gw.at[mine], gw.at[mine], g_s.at[10 + i], g_r.at[10 + i], (p, z)) for i, p in enumerate(plane)]
+
+    rows_end(0, e0)
+
+    for cp in g5:
+        cp.wait_recv()
+    mine = pl.ds(own, half)
+    g6 = send(gw.at[mine], gw.at[mine], g_s.at[13], g_r.at[13], (sib, z))
+
+    rows_end(1, e1)
+    f_cp = pltpu.make_async_copy(Fo, gf_o, loc_sem.at[6])
+    f_cp.start()
+    g6.wait_recv()
+    g_cp = pltpu.make_async_copy(gw, gw_o, loc_sem.at[7])
+    g_cp.start()
+    for cp in sent:
+        cp.wait_send()
+    hid_cp.wait()
+    f_cp.wait()
+    g_cp.wait()
+
+
+def fused(features, weight, cotangent, tiles, tile_count, tile_block):
+    blk, width = features.shape
+    secs, slots = tiles.shape[2], tiles.shape[3]
+    reps = lax.axis_size("rep")
+    chips = secs // 2
+    half = width // 2
+    piece = half // chips
+    sub = piece // reps
+    V = pltpu.VMEM
+    dma = pltpu.SemaphoreType.DMA
+    hbm = pl.BlockSpec(memory_space=pl.ANY)
+    smem = pl.BlockSpec(memory_space=pltpu.SMEM)
+    flops = 2 * 3 * 2 * (reps * blk) * (secs * blk) * width
+    return pl.pallas_call(
+        kernel,
+        out_shape=(jax.ShapeDtypeStruct((blk, width), F32), jax.ShapeDtypeStruct((width, width), F32),
+                   jax.ShapeDtypeStruct((blk, width), F32)),
+        in_specs=[hbm, hbm, hbm, hbm, smem, smem],
+        out_specs=(hbm, hbm, hbm),
+        scratch_shapes=[
+            V((2, secs, blk, blk), F32), V((secs, slots, blk, blk), F32), V((width, width), F32), V((blk, width), F32),
+            V((reps * blk, secs * blk), BF16), V((reps * blk, secs * blk), BF16),
+            V((secs * blk, reps * blk), BF16), V((secs * blk, reps * blk), BF16),
+            V((2, reps, blk, blk), F32), V((2, reps - 1, blk, blk), F32), V((2, reps, blk, blk), F32),
+            V((2, 2, chips, blk, blk), F32), V((2, chips, blk, blk), F32), V((2, 3, blk, blk), F32), V((2, 3, blk, blk), F32),
+            V((blk, width), F32), V((blk, width), F32),
+            V((width, width), F32), V((half, width), F32), V((half, width), F32), V((3, piece, width), F32),
+            V((piece, width), F32), V((reps - 1, sub, width), F32), V((width, width), F32),
+            dma((8,)), dma((2, 7)), dma((2, 7)), dma((2, 3)), dma((2, 3)), dma((2, 3)), dma((2, 3)),
+            dma((2, 4)), dma((2, 4)), dma((14,)), dma((14,)),
+        ],
+        compiler_params=pltpu.CompilerParams(collective_id=0, has_side_effects=True, vmem_limit_bytes=48 * 1024 * 1024),
+        cost_estimate=pl.CostEstimate(flops=flops, bytes_accessed=4 * tiles.size, transcendentals=blk * width),
+        name="graph_step",
+    )(features, weight, cotangent, tiles, tile_count, tile_block)
 
 
 def silu_slope(pre):
@@ -57,4 +325,5 @@
         P("rows", "rep", None, None),
     )
     out_specs = (P(("rows", "rep"), None), P(), P(("rows", "rep"), None))
-    return jax.shard_map(body, mesh=mesh, in_specs=in_specs, out_specs=out_specs, check_vma=False)
+    fits = mesh.shape["rows"] == 8 and mesh.shape["rep"] == 4
+    return jax.shard_map(fused if fits else body, mesh=mesh, in_specs=in_specs, out_specs=out_specs, check_vma=False)

time: 239 us -> 58.6 us (0.25)
  waiting for transfers between devices: 191 us -> 0 us
  Pallas kernels: 0 us -> 51 us
  blocking collectives: 15.9 us -> 0 us
  matrix products: 14.3 us -> 0 us
  between operations: 13.8 us -> 0.65 us
  local copies, waits for them, and re-layouts: 0.92 us -> 6.76 us
    psum x1 -> x0, waiting for transfers between devices: 104 us -> none  [body(): grad_weight = lax.psum(weight_term, ('rows', 'rep')) / math.sqrt(node_total)]
    reduce_scatter x2 -> x0, waiting for transfers between devices: 58.7 us -> none  [the longest x1 37 us: body(): lax.psum_scatter(all_terms, 'rows', scatter_dimension=0, tiled=True)]
    pallas_call x0 -> x1, Pallas kernels: none -> 51 us  [fused(): pl.pallas_call(kernel, out_shape=(jax.ShapeDtypeStruct((blk, width), F32)...]
    all_gather x1 -> x0, waiting for transfers between devices: 27.5 us -> none  [body(): lax.all_gather(features, 'rows', axis=0, tiled=True)]
    all_gather x1 -> x0, blocking collectives: 15.9 us -> none  [body(): lax.all_gather(back, 'rep', axis=0, tiled=True).reshape(groups, blk, width)]
    dot_general x7 -> x0, matrix products: 14.3 us -> none  [the longest x1 3.61 us: body(): result = jnp.einsum('stab,staf->sbf', tile_set, picked, precision=highest)]
    unnamed x8 -> x14, local copies, waits for them, and re-layouts: 0.03 us -> 6.76 us
  transfers between devices with their start and end apart: 4 -> 0, of which waited for: 4 -> 0; matrix products, arithmetic and copies ran while one was open for 3% -> 0% of each run, Pallas kernels for 0% -> 0%
where the time goes in v1:
time: 58.6 us; the launch traced here: 58.4 us
  Pallas kernels  51 us (87%)
  local copies, waits for them, and re-layouts  6.76 us (12%)
  between operations  0.65 us (1%)
    pallas_call x1, Pallas kernels, fused(): pl.pallas_call(kernel, out_shape=(jax.ShapeDtypeStruct((blk, width), F32)...  51 us
    unnamed x14, local copies, waits for them, and re-layouts  6.76 us

profile of v1, /device:TPU:0, one launch (start us, length us, event | category | flops | bytes accessed | tf_op | source)
XLA Modules:
  0.0 58.4 jit_solution(18079049908388203135)
XLA Ops:
  0.6 0.0 copy-start.4
  0.6 0.8 %copy.9.blks = s32[1,1,8,2]{3,2,1,0:T(8,128)S(1)} copy(s32[1,1,8,2]{2,3,1,0:T(2,128)} %param.11) | data formatting | bytes 128 | tf_op args[5]
  1.4 0.0 copy-done.4
  1.4 0.0 copy-start
  1.4 1.2 %copy-done = f32[1,1,8,2,128,128]{5,4,3,2,1,0:T(8,128)S(1)} copy-done((f32[1,1,8,2,128,128]{5,4,3,2,1,0:T(8,128)S(1)}, f32[1,1,8,2,128,128]{5,4,3,2,1,0:T(8,128)}, u32[]{:S(2)}) %copy-start) | copy-done | bytes 1048600
  2.6 0.0 copy-start.1
  2.6 0.9 %copy-done.1 = f32[256,256]{1,0:T(8,128)S(1)} copy-done((f32[256,256]{1,0:T(8,128)S(1)}, f32[256,256]{1,0:T(8,128)}, u32[]{:S(2)}) %copy-start.1) | copy-done | bytes 262168
  3.6 0.0 copy-start.2
  3.6 0.9 %copy-done.2 = f32[128,256]{1,0:T(8,128)S(1)} copy-done((f32[128,256]{1,0:T(8,128)S(1)}, f32[128,256]{1,0:T(8,128)}, u32[]{:S(2)}) %copy-start.2) | copy-done | bytes 131096
  4.5 0.0 copy-start.3
  4.5 0.9 %copy-done.3 = f32[128,256]{1,0:T(8,128)S(1)} copy-done((f32[128,256]{1,0:T(8,128)S(1)}, f32[128,256]{1,0:T(8,128)}, u32[]{:S(2)}) %copy-start.3) | copy-done | bytes 131096
  5.4 51.0 %graph_step.1 = (f32[128,256]{1,0:T(8,128)S(1)}, f32[256,256]{1,0:T(8,128)S(1)}, f32[128,256]{1,0:T(8,128)S(1)}) custom-call(f32[128,256]{1,0:T(8,128)S(1)} %copy-done.2, f32[256,256]{1,0:T(8,128)S(1)} %copy-done.1, f32[128,256]{1,0:T(8,128)S(1)} %copy-done.3, f32[1,1,8,2,128,128]{5,4,3,2,1,0:T(8,128)S(1)} %copy-done, s32[1,1,8]{2,1,0:T(1,128)S(1)} %copy-done.4, ...), custom_call_target="tpu_custom_call" | custom-call | flops 1610612736 | bytes 1048576 | tf_op jit(solution)/shard_map/graph_step/pallas_call | solution.py:253
  56.4 0.7 %copy.13 = f32[128,256]{1,0:T(8,128)} copy(f32[128,256]{1,0:T(8,128)S(1)} %get-tuple-element.6) | data formatting | bytes 262144
  57.0 0.7 %copy.14 = f32[256,256]{1,0:T(8,128)} copy(f32[256,256]{1,0:T(8,128)S(1)} %get-tuple-element.7) | data formatting | bytes 524288
  57.7 0.7 %copy.15 = f32[128,256]{1,0:T(8,128)} copy(f32[128,256]{1,0:T(8,128)S(1)} %get-tuple-element.8) | data formatting | bytes 262144
Async XLA Ops:
  0.6 0.8 %copy-start.4 = (s32[1,1,8]{2,1,0:T(1,128)S(1)}, s32[1,1,8]{2,1,0:T(1,128)}, u32[]{:S(2)}) copy-start(s32[1,1,8]{2,1,0:T(1,128)} %cnt.1) | copy-start | bytes 100
  1.4 1.2 %copy-start = (f32[1,1,8,2,128,128]{5,4,3,2,1,0:T(8,128)S(1)}, f32[1,1,8,2,128,128]{5,4,3,2,1,0:T(8,128)}, u32[]{:S(2)}) copy-start(f32[1,1,8,2,128,128]{5,4,3,2,1,0:T(8,128)} %tiles.1) | copy-start | bytes 3145732
  2.6 0.9 %copy-start.1 = (f32[256,256]{1,0:T(8,128)S(1)}, f32[256,256]{1,0:T(8,128)}, u32[]{:S(2)}) copy-start(f32[256,256]{1,0:T(8,128)} %weight.1) | copy-start | bytes 786436
  3.6 0.9 %copy-start.2 = (f32[128,256]{1,0:T(8,128)S(1)}, f32[128,256]{1,0:T(8,128)}, u32[]{:S(2)}) copy-start(f32[128,256]{1,0:T(8,128)} %feat.1) | copy-start | bytes 393220
  4.5 0.9 %copy-start.3 = (f32[128,256]{1,0:T(8,128)S(1)}, f32[128,256]{1,0:T(8,128)}, u32[]{:S(2)}) copy-start(f32[128,256]{1,0:T(8,128)} %cot.1) | copy-start | bytes 393220

commit v2 on v1

--- a/solution.py
+++ b/solution.py
@@ -8,6 +8,7 @@
 from jax.experimental.pallas import tpu as pltpu
 from jax.sharding import PartitionSpec as P
 
+LIMIT = 60 * 1024 * 1024
 MESH = pl.DeviceIdType.MESH
 F32 = jnp.float32
 BF16 = jnp.bfloat16
@@ -28,9 +29,9 @@
 
 
 def kernel(feat, weight, cot, tiles, cnt, blks, hid_o, gw_o, gf_o,
-           G, T, W, C, Ahi, Alo, AThi, ATlo, Pb, Rb, Bk, Rs, Es, Ec, Er, Ho, Fo,
+           G, T, W, C, Ahi, Alo, AThi, ATlo, Pb, Rb, St, Bk, Rs, Es, Ec, Er, Ho, Fo,
            wt, ws, wc, wr, wz, wzr, gw,
-           loc_sem, a_s, a_r, b_s, b_r, d_s, d_r, e_s, e_r, g_s, g_r):
+           loc_sem, a_s, a_r, b_s, b_r, st_r, d_s, d_r, e_s, e_r, g_s, g_r):
     blk = T.shape[2]
     secs = T.shape[0]
     reps = Pb.shape[1]
@@ -48,6 +49,11 @@
     dg = xn + yn - row
     plane = (xn, yn, dg)
     zs = [(z + d) % reps for d in range(1, reps)]
+    near = z + 1 - 2 * (z % 2)
+    far = (z + 2) % reps
+    mir = reps - 1 - z
+    inner = (z == 1) | (z == 2)
+    outer = (z == 0) | (z == 3)
 
     barrier = pltpu.get_barrier_semaphore()
     peers = [(sib, z)] + [(p, z) for p in plane] + [(row, k) for k in zs]
@@ -63,6 +69,10 @@
 
     sent = []
 
+    def put(src, dst, ss, rs, dev):
+        return pltpu.make_async_remote_copy(src_ref=src, dst_ref=dst, send_sem=ss, recv_sem=rs,
+                                            device_id=dev, device_id_type=MESH)
+
     def send(src, dst, ss, rs, dev):
         cp = pltpu.make_async_remote_copy(src_ref=src, dst_ref=dst, send_sem=ss, recv_sem=rs,
                                           device_id=dev, device_id_type=MESH)
@@ -94,13 +104,27 @@
             Ahi[k * blk:(k + 1) * blk, cols] = hi
             Alo[k * blk:(k + 1) * blk, cols] = lo
 
-    b_cp = []
+    def b_put(h, k, slot, dev):
+        return put(Pb.at[h, k], Rb.at[h, slot], b_s.at[h, slot], b_r.at[h, slot], (row, dev))
+
+    def stage_put(h):
+        return put(Pb.at[h, mir], St.at[h], b_s.at[h, 2], st_r.at[h], (row, near))
+
+    def combine(h):
+        @pl.when(inner)
+        def _():
+            stage_put(h).wait_recv()
+            Pb[h, far] = Pb[h, far] + St[h]
+            b_put(h, far, 1, far).start()
+
     for h in range(2):
         fwd = []
         for i, p in enumerate(plane):
             a_cp[h][i].wait_recv()
             fwd.append(send(G.at[h, p], G.at[h, p], a_s.at[h, 4 + i], a_r.at[h, 4 + i], (sib, z)))
         a_cp[h][3].wait_recv()
+        if h == 1:
+            combine(0)
         for cp in fwd:
             cp.wait_recv()
         fh, fl = split(G[h].reshape(secs * blk, blk))
@@ -108,7 +132,17 @@
         acc = mm(Ahi[...], rhs)
         acc = acc[:, :blk] + (acc[:, blk:] + mm(Alo[...], fh))
         Pb[h] = acc.reshape(reps, blk, blk)
-        b_cp.append([send(Pb.at[h, k], Rb.at[h, i], b_s.at[h, i], b_r.at[h, i], (row, k)) for i, k in enumerate(zs)])
+
+        @pl.when(outer)
+        def _():
+            stage_put(h).start()
+            b_put(h, far, 1, far).start()
+            b_put(h, near, 0, near).start()
+
+        @pl.when(inner)
+        def _():
+            b_put(h, mir, 2, mir).start()
+            b_put(h, near, 0, near).start()
 
     @pl.loop(0, secs)
     def _(s):
@@ -123,29 +157,56 @@
             AThi[rows, k * blk:(k + 1) * blk] = hi
             ATlo[rows, k * blk:(k + 1) * blk] = lo
 
+    combine(1)
     loads[3].wait()
     loads[4].wait()
     agg = []
     for h in range(2):
-        part = Pb[h, z]
-        for i in range(reps - 1):
-            b_cp[h][i].wait_recv()
-            part = part + Rb[h, i]
-        agg.append(part)
+        b_put(h, near, 0, near).wait_recv()
+        part = Pb[h, z] + Rb[h, 0]
+
+        @pl.when(inner)
+        def _():
+            b_put(h, mir, 2, mir).wait_recv()
+
+        @pl.when(outer)
+        def _():
+            Rb[h, 2] = jnp.zeros_like(Rb[h, 2])
+
+        part = part + Rb[h, 2]
+        b_put(h, far, 1, far).wait_recv()
+        agg.append(part + Rb[h, 1])
     agg = jnp.concatenate(agg, axis=1)
     w = W[...]
     pre = mm3(agg, w)
     sig = 1.0 / (1.0 + jnp.exp(-pre))
     delta = C[...] * (sig * (1.0 + pre * (1.0 - sig)))
     back = mm3(delta, w, ((1,), (1,)))
-    d_cp = []
+
+    def d_put(h, k, slot, dev):
+        return put(Bk.at[h, k], Bk.at[h, k], d_s.at[h, slot], d_r.at[h, slot], (row, dev))
+
     for h in range(2):
         Bk[h, z] = back[:, h * blk:(h + 1) * blk]
-        mine = Bk.at[h, z]
-        d_cp.append([send(mine, mine, d_s.at[h, i], d_r.at[h, i], (row, k)) for i, k in enumerate(zs)])
+        d_put(h, z, 2, mir).start()
+
+        @pl.when(outer)
+        def _():
+            d_put(h, z, 1, far).start()
+
+        d_put(h, z, 0, near).start()
+
+    def relay(h):
+        @pl.when(inner)
+        def _():
+            d_put(h, mir, 2, mir).wait_recv()
+            d_put(h, mir, 1, near).start()
+
     Ho[...] = pre * sig
     hid_cp = pltpu.make_async_copy(Ho, hid_o, loc_sem.at[5])
     hid_cp.start()
+
+    relay(0)
 
     wt[...] = mm3(agg.T, delta) * (1.0 / math.sqrt(blk * secs * reps))
     half = wt.shape[0] // 2
@@ -160,8 +221,13 @@
           for i, p in enumerate(plane)]
 
     def rows_start(h):
-        for cp in d_cp[h]:
-            cp.wait_recv()
+        d_put(h, near, 0, near).wait_recv()
+        d_put(h, far, 1, far).wait_recv()
+
+        @pl.when(outer)
+        def _():
+            d_put(h, mir, 2, mir).wait_recv()
+
         bh, bl = split(Bk[h].reshape(quarter, blk))
         rhs = jnp.concatenate([bh, bl], axis=1)
         out = None
@@ -171,15 +237,17 @@
             acc = acc[:, :blk] + (acc[:, blk:] + mm(ATlo[at], bh))
             Rs[h, 0 if first else 1] = acc.reshape(chips, blk, blk)
             if first:
-                out = send(Rs.at[h, 0], Es.at[h], e_s.at[h, 0], e_r.at[h, 0], (sib, z))
+                out = [send(Rs.at[h, 0, p // 2], Es.at[h, p // 2], e_s.at[h, 3 + i], e_r.at[h, 3 + i], (sib, z))
+                       for i, p in enumerate((dg, xn, yn, row))]
         return out
 
-    def rows_mid(h, cp):
-        cp.wait_recv()
+    def rows_mid(h, cps):
         out = []
         for i, p in enumerate((dg, xn, yn)):
+            cps[i].wait_recv()
             Ec[h, i] = Rs[h, 1, p // 2] + Es[h, p // 2]
-            out.append(send(Ec.at[h, i], Er.at[h, i], e_s.at[h, 1 + i], e_r.at[h, 1 + i], (p, z)))
+            out.append(send(Ec.at[h, i], Er.at[h, i], e_s.at[h, i], e_r.at[h, i], (p, z)))
+        cps[3].wait_recv()
         return out
 
     def rows_end(h, cps):
@@ -190,6 +258,7 @@
         Fo[:, h * blk:(h + 1) * blk] = total
 
     e0 = rows_start(0)
+    relay(1)
     e0 = rows_mid(0, e0)
 
     at = pl.multiple_of(q * piece, piece)
@@ -232,9 +301,21 @@
     g_cp.start()
     for cp in sent:
         cp.wait_send()
+    for h in range(2):
+        for i in range(3):
+            b_put(h, z, i, near).wait_send()
+            d_put(h, z, i, near).wait_send()
     hid_cp.wait()
     f_cp.wait()
     g_cp.wait()
+
+
+def store(a, b, c, x, y, z, sem):
+    cps = [pltpu.make_async_copy(s, d, sem.at[i]) for i, (s, d) in enumerate(((a, x), (b, y), (c, z)))]
+    for cp in cps:
+        cp.start()
+    for cp in cps:
+        cp.wait()
 
 
 def fused(features, weight, cotangent, tiles, tile_count, tile_block):
@@ -250,7 +331,7 @@
     hbm = pl.BlockSpec(memory_space=pl.ANY)
     smem = pl.BlockSpec(memory_space=pltpu.SMEM)
     flops = 2 * 3 * 2 * (reps * blk) * (secs * blk) * width
-    return pl.pallas_call(
+    raw = pl.pallas_call(
         kernel,
         out_shape=(jax.ShapeDtypeStruct((blk, width), F32), jax.ShapeDtypeStruct((width, width), F32),
                    jax.ShapeDtypeStruct((blk, width), F32)),
@@ -260,18 +341,27 @@
             V((2, secs, blk, blk), F32), V((secs, slots, blk, blk), F32), V((width, width), F32), V((blk, width), F32),
             V((reps * blk, secs * blk), BF16), V((reps * blk, secs * blk), BF16),
             V((secs * blk, reps * blk), BF16), V((secs * blk, reps * blk), BF16),
-            V((2, reps, blk, blk), F32), V((2, reps - 1, blk, blk), F32), V((2, reps, blk, blk), F32),
+            V((2, reps, blk, blk), F32), V((2, reps - 1, blk, blk), F32), V((2, blk, blk), F32), V((2, reps, blk, blk), F32),
             V((2, 2, chips, blk, blk), F32), V((2, chips, blk, blk), F32), V((2, 3, blk, blk), F32), V((2, 3, blk, blk), F32),
             V((blk, width), F32), V((blk, width), F32),
             V((width, width), F32), V((half, width), F32), V((half, width), F32), V((3, piece, width), F32),
             V((piece, width), F32), V((reps - 1, sub, width), F32), V((width, width), F32),
-            dma((8,)), dma((2, 7)), dma((2, 7)), dma((2, 3)), dma((2, 3)), dma((2, 3)), dma((2, 3)),
-            dma((2, 4)), dma((2, 4)), dma((14,)), dma((14,)),
+            dma((8,)), dma((2, 7)), dma((2, 7)), dma((2, 3)), dma((2, 3)), dma((2,)), dma((2, 3)), dma((2, 3)),
+            dma((2, 7)), dma((2, 7)), dma((14,)), dma((14,)),
         ],
-        compiler_params=pltpu.CompilerParams(collective_id=0, has_side_effects=True, vmem_limit_bytes=48 * 1024 * 1024),
+        compiler_params=pltpu.CompilerParams(collective_id=0, has_side_effects=True, vmem_limit_bytes=LIMIT),
         cost_estimate=pl.CostEstimate(flops=flops, bytes_accessed=4 * tiles.size, transcendentals=blk * width),
         name="graph_step",
     )(features, weight, cotangent, tiles, tile_count, tile_block)
+    return pl.pallas_call(
+        store,
+        out_shape=tuple(jax.ShapeDtypeStruct(r.shape, r.dtype) for r in raw),
+        in_specs=[hbm] * 3,
+        out_specs=(hbm,) * 3,
+        scratch_shapes=[dma((3,))],
+        compiler_params=pltpu.CompilerParams(vmem_limit_bytes=LIMIT),
+        name="store_results",
+    )(*raw)
 
 
 def silu_slope(pre):

time: 58.6 us -> 68 us (1.16)
  Pallas kernels: 51 us -> 65.3 us
  local copies, waits for them, and re-layouts: 6.76 us -> 1.35 us
    pallas_call x0 -> x1, Pallas kernels: none -> 17 us  [fused(): pl.pallas_call(store, out_shape=tuple((jax.ShapeDtypeStruct(r.shape, r.dt...]
    unnamed x14 -> x1, local copies, waits for them, and re-layouts: 6.76 us -> 1.35 us
    pallas_call x1, Pallas kernels: 51 us -> 48.3 us  [fused(): pl.pallas_call(kernel, out_shape=(jax.ShapeDtypeStruct((blk, width), F32)...]
where the time goes in v2:
time: 68 us; the launch traced here: 67.3 us
  Pallas kernels  65.3 us (96%)
  local copies, waits for them, and re-layouts  1.35 us (2%)
    pallas_call x1, Pallas kernels, fused(): pl.pallas_call(kernel, out_shape=(jax.ShapeDtypeStruct((blk, width), F32)...  48.3 us
    pallas_call x1, Pallas kernels, fused(): pl.pallas_call(store, out_shape=tuple((jax.ShapeDtypeStruct(r.shape, r.dt...  17 us

profile of v2, /device:TPU:0, one launch (start us, length us, event | category | flops | bytes accessed | tf_op | source)
XLA Modules:
  0.0 67.3 jit_solution(7913590326375362967)
XLA Ops:
  0.6 1.3 %copy.9.blks = s32[1,1,8,2]{3,2,1,0:T(8,128)} copy(s32[1,1,8,2]{2,3,1,0:T(2,128)} %param.11) | data formatting | bytes 128 | tf_op args[5]
  2.0 48.3 %graph_step.1 = (f32[128,256]{1,0:T(8,128)}, f32[256,256]{1,0:T(8,128)}, f32[128,256]{1,0:T(8,128)}) custom-call(f32[128,256]{1,0:T(8,128)} %feat.1, f32[256,256]{1,0:T(8,128)} %weight.1, f32[128,256]{1,0:T(8,128)} %cot.1, f32[1,1,8,2,128,128]{5,4,3,2,1,0:T(8,128)} %tiles.1, s32[1,1,8]{2,1,0:T(1,128)} %cnt.1, s32[1,1,8,2]{3,2,1,0:T(8,128)} %copy.9.blks), custom_call_target="tpu_custom_call" | custom-call | flops 1610612736 | bytes 1048576 | tf_op jit(solution)/shard_map/graph_step/pallas_call | solution.py:334
  50.3 17.0 %store_results.1 = (f32[128,256]{1,0:T(8,128)}, f32[256,256]{1,0:T(8,128)}, f32[128,256]{1,0:T(8,128)}) custom-call(f32[128,256]{1,0:T(8,128)} %get-tuple-element.6.a, f32[256,256]{1,0:T(8,128)} %get-tuple-element.7.b, f32[128,256]{1,0:T(8,128)} %get-tuple-element.8.c), custom_call_target="tpu_custom_call" | custom-call | tf_op jit(solution)/shard_map/store_results/pallas_call | solution.py:356

commit v3 on v2

--- a/solution.py
+++ b/solution.py
@@ -47,7 +47,7 @@
     xn = row + 2 - 4 * x
     yn = row + 4 - 8 * y
     dg = xn + yn - row
-    plane = (xn, yn, dg)
+    plane = (dg, xn, yn)
     zs = [(z + d) % reps for d in range(1, reps)]
     near = z + 1 - 2 * (z % 2)
     far = (z + 2) % reps
@@ -81,10 +81,13 @@
         return cp
 
     a_cp = []
-    for h in range(2):
+
+    def gather(h):
         loads[h].wait()
         mine = G.at[h, row]
-        a_cp.append([send(mine, mine, a_s.at[h, i], a_r.at[h, i], (p, z)) for i, p in enumerate((xn, yn, dg, sib))])
+        a_cp.append([send(mine, mine, a_s.at[h, i], a_r.at[h, i], (p, z)) for i, p in enumerate((dg, xn, yn, sib))])
+
+    gather(0)
 
     loads[2].wait()
 
@@ -104,18 +107,55 @@
             Ahi[k * blk:(k + 1) * blk, cols] = hi
             Alo[k * blk:(k + 1) * blk, cols] = lo
 
-    def b_put(h, k, slot, dev):
-        return put(Pb.at[h, k], Rb.at[h, slot], b_s.at[h, slot], b_r.at[h, slot], (row, dev))
-
-    def stage_put(h):
-        return put(Pb.at[h, mir], St.at[h], b_s.at[h, 2], st_r.at[h], (row, near))
-
-    def combine(h):
+    rh = blk // 2
+    b_pc = ((0, 0, blk), (1, 0, rh), (1, rh, rh))
+    d_pc = ((0, 0, rh), (0, rh, rh), (1, 0, blk))
+
+    def b_put(n, k, slot, dev):
+        h, at, size = b_pc[n]
+        return put(Pb.at[h, k, at:at + size], Rb.at[h, slot, at:at + size], b_s.at[n, slot], b_r.at[n, slot], (row, dev))
+
+    def stage_put(n):
+        h, at, size = b_pc[n]
+        return put(Pb.at[h, mir, at:at + size], St.at[h, at:at + size], b_s.at[n, 2], st_r.at[n], (row, near))
+
+    def b_send(n):
+        @pl.when(outer)
+        def _():
+            stage_put(n).start()
+            b_put(n, far, 1, far).start()
+            b_put(n, near, 0, near).start()
+
         @pl.when(inner)
         def _():
-            stage_put(h).wait_recv()
-            Pb[h, far] = Pb[h, far] + St[h]
-            b_put(h, far, 1, far).start()
+            b_put(n, mir, 2, mir).start()
+            b_put(n, near, 0, near).start()
+
+    def combine(n):
+        h, at, size = b_pc[n]
+
+        @pl.when(inner)
+        def _():
+            stage_put(n).wait_recv()
+            Pb[h, far, at:at + size] = Pb[h, far, at:at + size] + St[h, at:at + size]
+            b_put(n, far, 1, far).start()
+
+    def b_sum(n):
+        h, at, size = b_pc[n]
+        b_put(n, near, 0, near).wait_recv()
+        part = Pb[h, z, at:at + size] + Rb[h, 0, at:at + size]
+
+        @pl.when(inner)
+        def _():
+            b_put(n, mir, 2, mir).wait_recv()
+
+        @pl.when(outer)
+        def _():
+            Rb[h, 2, at:at + size] = jnp.zeros((size, blk), F32)
+
+        part = part + Rb[h, 2, at:at + size]
+        b_put(n, far, 1, far).wait_recv()
+        return part + Rb[h, 1, at:at + size]
 
     for h in range(2):
         fwd = []
@@ -123,7 +163,9 @@
             a_cp[h][i].wait_recv()
             fwd.append(send(G.at[h, p], G.at[h, p], a_s.at[h, 4 + i], a_r.at[h, 4 + i], (sib, z)))
         a_cp[h][3].wait_recv()
-        if h == 1:
+        if h == 0:
+            gather(1)
+        else:
             combine(0)
         for cp in fwd:
             cp.wait_recv()
@@ -132,17 +174,8 @@
         acc = mm(Ahi[...], rhs)
         acc = acc[:, :blk] + (acc[:, blk:] + mm(Alo[...], fh))
         Pb[h] = acc.reshape(reps, blk, blk)
-
-        @pl.when(outer)
-        def _():
-            stage_put(h).start()
-            b_put(h, far, 1, far).start()
-            b_put(h, near, 0, near).start()
-
-        @pl.when(inner)
-        def _():
-            b_put(h, mir, 2, mir).start()
-            b_put(h, near, 0, near).start()
+        for n in ((0,), (1, 2))[h]:
+            b_send(n)
 
     @pl.loop(0, secs)
     def _(s):
@@ -158,55 +191,53 @@
             ATlo[rows, k * blk:(k + 1) * blk] = lo
 
     combine(1)
+    combine(2)
     loads[3].wait()
     loads[4].wait()
-    agg = []
-    for h in range(2):
-        b_put(h, near, 0, near).wait_recv()
-        part = Pb[h, z] + Rb[h, 0]
-
-        @pl.when(inner)
-        def _():
-            b_put(h, mir, 2, mir).wait_recv()
+
+    def d_put(n, k, slot, dev):
+        h, at, size = d_pc[n]
+        ref = Bk.at[h, k, at:at + size]
+        return put(ref, ref, d_s.at[n, slot], d_r.at[n, slot], (row, dev))
+
+    def d_send(n):
+        d_put(n, z, 2, mir).start()
 
         @pl.when(outer)
         def _():
-            Rb[h, 2] = jnp.zeros_like(Rb[h, 2])
-
-        part = part + Rb[h, 2]
-        b_put(h, far, 1, far).wait_recv()
-        agg.append(part + Rb[h, 1])
-    agg = jnp.concatenate(agg, axis=1)
+            d_put(n, z, 1, far).start()
+
+        d_put(n, z, 0, near).start()
+
     w = W[...]
-    pre = mm3(agg, w)
-    sig = 1.0 / (1.0 + jnp.exp(-pre))
-    delta = C[...] * (sig * (1.0 + pre * (1.0 - sig)))
-    back = mm3(delta, w, ((1,), (1,)))
-
-    def d_put(h, k, slot, dev):
-        return put(Bk.at[h, k], Bk.at[h, k], d_s.at[h, slot], d_r.at[h, slot], (row, dev))
-
-    for h in range(2):
-        Bk[h, z] = back[:, h * blk:(h + 1) * blk]
-        d_put(h, z, 2, mir).start()
-
-        @pl.when(outer)
-        def _():
-            d_put(h, z, 1, far).start()
-
-        d_put(h, z, 0, near).start()
-
-    def relay(h):
-        @pl.when(inner)
-        def _():
-            d_put(h, mir, 2, mir).wait_recv()
-            d_put(h, mir, 1, near).start()
-
-    Ho[...] = pre * sig
+    agg0 = b_sum(0)
+    pre0 = mm3(agg0, w[:blk])
+    agg1, delta = [], []
+    for n in (1, 2):
+        at = b_pc[n][1]
+        agg1.append(b_sum(n))
+        pre = pre0[at:at + rh] + mm3(agg1[-1], w[blk:])
+        sig = 1.0 / (1.0 + jnp.exp(-pre))
+        delta.append(C[at:at + rh] * (sig * (1.0 + pre * (1.0 - sig))))
+        back = mm3(delta[-1], w, ((1,), (1,)))
+        for h in range(2):
+            Bk[h, z, at:at + rh] = back[:, h * blk:(h + 1) * blk]
+        d_send(n - 1)
+        Ho[at:at + rh] = pre * sig
+    d_send(2)
+    agg = jnp.concatenate([agg0, jnp.concatenate(agg1, axis=0)], axis=1)
+    delta = jnp.concatenate(delta, axis=0)
     hid_cp = pltpu.make_async_copy(Ho, hid_o, loc_sem.at[5])
     hid_cp.start()
 
+    def relay(n):
+        @pl.when(inner)
+        def _():
+            d_put(n, mir, 2, mir).wait_recv()
+            d_put(n, mir, 1, near).start()
+
     relay(0)
+    relay(1)
 
     wt[...] = mm3(agg.T, delta) * (1.0 / math.sqrt(blk * secs * reps))
     half = wt.shape[0] // 2
@@ -221,12 +252,14 @@
           for i, p in enumerate(plane)]
 
     def rows_start(h):
-        d_put(h, near, 0, near).wait_recv()
-        d_put(h, far, 1, far).wait_recv()
+        for n in ((0, 1), (2,))[h]:
+            d_put(n, near, 0, near).wait_recv()
+            d_put(n, far, 1, far).wait_recv()
 
         @pl.when(outer)
         def _():
-            d_put(h, mir, 2, mir).wait_recv()
+            for n in ((0, 1), (2,))[h]:
+                d_put(n, mir, 2, mir).wait_recv()
 
         bh, bl = split(Bk[h].reshape(quarter, blk))
         rhs = jnp.concatenate([bh, bl], axis=1)
@@ -258,7 +291,7 @@
         Fo[:, h * blk:(h + 1) * blk] = total
 
     e0 = rows_start(0)
-    relay(1)
+    relay(2)
     e0 = rows_mid(0, e0)
 
     at = pl.multiple_of(q * piece, piece)
@@ -301,21 +334,26 @@
     g_cp.start()
     for cp in sent:
         cp.wait_send()
-    for h in range(2):
+    for n in range(3):
         for i in range(3):
-            b_put(h, z, i, near).wait_send()
-            d_put(h, z, i, near).wait_send()
+            b_put(n, z, i, near).wait_send()
+            d_put(n, z, i, near).wait_send()
     hid_cp.wait()
     f_cp.wait()
     g_cp.wait()
 
 
-def store(a, b, c, x, y, z, sem):
-    cps = [pltpu.make_async_copy(s, d, sem.at[i]) for i, (s, d) in enumerate(((a, x), (b, y), (c, z)))]
-    for cp in cps:
+def store(a, b, c, x, y, z, u, v, w, sem):
+    bufs = ((a, u, x), (b, v, y), (c, w, z))
+    ins = [pltpu.make_async_copy(s, t, sem.at[0, i]) for i, (s, t, _) in enumerate(bufs)]
+    outs = [pltpu.make_async_copy(t, d, sem.at[1, i]) for i, (_, t, d) in enumerate(bufs)]
+    for cp in ins:
         cp.start()
-    for cp in cps:
+    for cp, out in zip(ins, outs):
         cp.wait()
+        out.start()
+    for out in outs:
+        out.wait()
 
 
 def fused(features, weight, cotangent, tiles, tile_count, tile_block):
@@ -328,7 +366,7 @@
     sub = piece // reps
     V = pltpu.VMEM
     dma = pltpu.SemaphoreType.DMA
-    hbm = pl.BlockSpec(memory_space=pl.ANY)
+    hbm = pl.BlockSpec(memory_space=pltpu.HBM)
     smem = pl.BlockSpec(memory_space=pltpu.SMEM)
     flops = 2 * 3 * 2 * (reps * blk) * (secs * blk) * width
     raw = pl.pallas_call(
@@ -336,7 +374,7 @@
         out_shape=(jax.ShapeDtypeStruct((blk, width), F32), jax.ShapeDtypeStruct((width, width), F32),
                    jax.ShapeDtypeStruct((blk, width), F32)),
         in_specs=[hbm, hbm, hbm, hbm, smem, smem],
-        out_specs=(hbm, hbm, hbm),
+        out_specs=(hbm,) * 3,
         scratch_shapes=[
             V((2, secs, blk, blk), F32), V((secs, slots, blk, blk), F32), V((width, width), F32), V((blk, width), F32),
             V((reps * blk, secs * blk), BF16), V((reps * blk, secs * blk), BF16),
@@ -346,7 +384,7 @@
             V((blk, width), F32), V((blk, width), F32),
             V((width, width), F32), V((half, width), F32), V((half, width), F32), V((3, piece, width), F32),
             V((piece, width), F32), V((reps - 1, sub, width), F32), V((width, width), F32),
-            dma((8,)), dma((2, 7)), dma((2, 7)), dma((2, 3)), dma((2, 3)), dma((2,)), dma((2, 3)), dma((2, 3)),
+            dma((8,)), dma((2, 7)), dma((2, 7)), dma((3, 3)), dma((3, 3)), dma((3,)), dma((3, 3)), dma((3, 3)),
             dma((2, 7)), dma((2, 7)), dma((14,)), dma((14,)),
         ],
         compiler_params=pltpu.CompilerParams(collective_id=0, has_side_effects=True, vmem_limit_bytes=LIMIT),
@@ -358,7 +396,7 @@
         out_shape=tuple(jax.ShapeDtypeStruct(r.shape, r.dtype) for r in raw),
         in_specs=[hbm] * 3,
         out_specs=(hbm,) * 3,
-        scratch_shapes=[dma((3,))],
+        scratch_shapes=[V(r.shape, r.dtype) for r in raw] + [dma((2, 3))],
         compiler_params=pltpu.CompilerParams(vmem_limit_bytes=LIMIT),
         name="store_results",
     )(*raw)

time: 68 us -> 51.4 us (0.76)
  Pallas kernels: 65.3 us -> 48.7 us
    pallas_call x1, Pallas kernels: 17 us -> 1.81 us  [fused(): pl.pallas_call(store, out_shape=tuple((jax.ShapeDtypeStruct(r.shape, r.dt...]
    pallas_call x1, Pallas kernels: 48.3 us -> 46.9 us  [fused(): pl.pallas_call(kernel, out_shape=(jax.ShapeDtypeStruct((blk, width), F32)...]
where the time goes in v3:
time: 51.4 us; the launch traced here: 50.7 us
  Pallas kernels  48.7 us (95%)
  local copies, waits for them, and re-layouts  1.35 us (3%)
  between operations  0.64 us (1%)
    pallas_call x1, Pallas kernels, fused(): pl.pallas_call(kernel, out_shape=(jax.ShapeDtypeStruct((blk, width), F32)...  46.9 us
    pallas_call x1, Pallas kernels, fused(): pl.pallas_call(store, out_shape=tuple((jax.ShapeDtypeStruct(r.shape, r.dt...  1.81 us
    unnamed x1, local copies, waits for them, and re-layouts  1.35 us

profile of v3, /device:TPU:0, one launch (start us, length us, event | category | flops | bytes accessed | tf_op | source)
XLA Modules:
  0.0 50.7 jit_solution(6781028391974843129)
XLA Ops:
  0.6 1.3 %copy.9.blks = s32[1,1,8,2]{3,2,1,0:T(8,128)} copy(s32[1,1,8,2]{2,3,1,0:T(2,128)} %param.11) | data formatting | bytes 128 | tf_op args[5]
  2.0 46.9 %graph_step.1 = (f32[128,256]{1,0:T(8,128)}, f32[256,256]{1,0:T(8,128)}, f32[128,256]{1,0:T(8,128)}) custom-call(f32[128,256]{1,0:T(8,128)} %feat.1, f32[256,256]{1,0:T(8,128)} %weight.1, f32[128,256]{1,0:T(8,128)} %cot.1, f32[1,1,8,2,128,128]{5,4,3,2,1,0:T(8,128)} %tiles.1, s32[1,1,8]{2,1,0:T(1,128)} %cnt.1, s32[1,1,8,2]{3,2,1,0:T(8,128)} %copy.9.blks), custom_call_target="tpu_custom_call" | custom-call | flops 1610612736 | bytes 1048576 | tf_op jit(solution)/shard_map/graph_step/pallas_call | solution.py:372
  48.9 1.8 %store_results.1 = (f32[128,256]{1,0:T(8,128)}, f32[256,256]{1,0:T(8,128)}, f32[128,256]{1,0:T(8,128)}) custom-call(f32[128,256]{1,0:T(8,128)} %get-tuple-element.6.a, f32[256,256]{1,0:T(8,128)} %get-tuple-element.7.b, f32[128,256]{1,0:T(8,128)} %get-tuple-element.8.c), custom_call_target="tpu_custom_call" | custom-call | tf_op jit(solution)/shard_map/store_results/pallas_call | solution.py:394

commit v4 on v3

--- a/solution.py
+++ b/solution.py
@@ -93,7 +93,7 @@
 
     def masks(s, k):
         n = cnt[0, 0, s]
-        return [jnp.where((blks[0, 0, s, t] == k) & (t < n), 1.0, 0.0).astype(F32) for t in range(T.shape[1])]
+        return [jnp.where((blks[0, 0, t, s] == k) & (t < n), 1.0, 0.0).astype(F32) for t in range(T.shape[1])]
 
     @pl.loop(0, secs)
     def _(s):
@@ -159,7 +159,7 @@
 
     for h in range(2):
         fwd = []
-        for i, p in enumerate(plane):
+        for i, p in ((1, xn), (2, yn), (0, dg)):
             a_cp[h][i].wait_recv()
             fwd.append(send(G.at[h, p], G.at[h, p], a_s.at[h, 4 + i], a_r.at[h, 4 + i], (sib, z)))
         a_cp[h][3].wait_recv()
@@ -236,8 +236,6 @@
             d_put(n, mir, 2, mir).wait_recv()
             d_put(n, mir, 1, near).start()
 
-    relay(0)
-    relay(1)
 
     wt[...] = mm3(agg.T, delta) * (1.0 / math.sqrt(blk * secs * reps))
     half = wt.shape[0] // 2
@@ -246,6 +244,8 @@
     oth = pl.multiple_of((1 - c) * half, half)
     own = pl.multiple_of(c * half, half)
     g1 = send(wt.at[pl.ds(oth, half)], ws, g_s.at[0], g_r.at[0], (sib, z))
+    relay(0)
+    relay(1)
     g1.wait_recv()
     wc[...] = wt[pl.ds(own, half)] + ws[...]
     g2 = [send(wc.at[pl.ds(pl.multiple_of((p // 2) * piece, piece), piece)], wr.at[i], g_s.at[1 + i], g_r.at[1 + i], (p, z))
@@ -303,9 +303,6 @@
     g3 = [send(wz.at[pl.ds(pl.multiple_of(k * sub, sub), sub)], wzr.at[i], g_s.at[4 + i], g_r.at[4 + i], (row, k))
           for i, k in enumerate(zs)]
 
-    e1 = rows_start(1)
-    e1 = rows_mid(1, e1)
-
     total = wz[pl.ds(pl.multiple_of(z * sub, sub), sub)]
     for i in range(reps - 1):
         g3[i].wait_recv()
@@ -314,11 +311,13 @@
     mine = pl.ds(pl.multiple_of(top + z * sub, sub), sub)
     gw[mine] = total
     g4 = [send(gw.at[mine], gw.at[mine], g_s.at[7 + i], g_r.at[7 + i], (row, k)) for i, k in enumerate(zs)]
+    e1 = rows_start(1)
     for cp in g4:
         cp.wait_recv()
     mine = pl.ds(pl.multiple_of(top, piece), piece)
     g5 = [send(gw.at[mine], gw.at[mine], g_s.at[10 + i], g_r.at[10 + i], (p, z)) for i, p in enumerate(plane)]
 
+    e1 = rows_mid(1, e1)
     rows_end(0, e0)
 
     for cp in g5:
@@ -390,7 +389,7 @@
         compiler_params=pltpu.CompilerParams(collective_id=0, has_side_effects=True, vmem_limit_bytes=LIMIT),
         cost_estimate=pl.CostEstimate(flops=flops, bytes_accessed=4 * tiles.size, transcendentals=blk * width),
         name="graph_step",
-    )(features, weight, cotangent, tiles, tile_count, tile_block)
+    )(features, weight, cotangent, tiles, tile_count, tile_block.transpose(0, 1, 3, 2))
     return pl.pallas_call(
         store,
         out_shape=tuple(jax.ShapeDtypeStruct(r.shape, r.dtype) for r in raw),

time: 51.4 us -> 49.4 us (0.961); the launches traced: 50.7 us -> 49.2 us
  local copies, waits for them, and re-layouts: 1.35 us -> 0 us
    unnamed x1 -> x0, local copies, waits for them, and re-layouts: 1.35 us -> none
where the time goes in v4:
time: 49.4 us; the launch traced here: 49.2 us
  Pallas kernels  48.6 us (98%)
  between operations  0.64 us (1%)
    pallas_call x1, Pallas kernels, fused(): pl.pallas_call(kernel, out_shape=(jax.ShapeDtypeStruct((blk, width), F32)...  46.8 us
    pallas_call x1, Pallas kernels, fused(): pl.pallas_call(store, out_shape=tuple((jax.ShapeDtypeStruct(r.shape, r.dt...  1.81 us

profile of v4, /device:TPU:0, one launch (start us, length us, event | category | flops | bytes accessed | tf_op | source)
XLA Modules:
  0.0 49.2 jit_solution(7359580770985836094)
XLA Ops:
  0.6 46.8 %graph_step.1 = (f32[128,256]{1,0:T(8,128)}, f32[256,256]{1,0:T(8,128)}, f32[128,256]{1,0:T(8,128)}) custom-call(f32[128,256]{1,0:T(8,128)} %feat.1, f32[256,256]{1,0:T(8,128)} %weight.1, f32[128,256]{1,0:T(8,128)} %cot.1, f32[1,1,8,2,128,128]{5,4,3,2,1,0:T(8,128)} %tiles.1, s32[1,1,8]{2,1,0:T(1,128)} %cnt.1, s32[1,1,2,8]{3,2,1,0:T(2,128)} %bitcast.1), custom_call_target="tpu_custom_call" | custom-call | flops 1610612736 | bytes 1048576 | tf_op jit(solution)/shard_map/graph_step/pallas_call | solution.py:371
  47.4 1.8 %store_results.1 = (f32[128,256]{1,0:T(8,128)}, f32[256,256]{1,0:T(8,128)}, f32[128,256]{1,0:T(8,128)}) custom-call(f32[128,256]{1,0:T(8,128)} %get-tuple-element.6.a, f32[256,256]{1,0:T(8,128)} %get-tuple-element.7.b, f32[128,256]{1,0:T(8,128)} %get-tuple-element.8.c), custom_call_target="tpu_custom_call" | custom-call | tf_op jit(solution)/shard_map/store_results/pallas_call | solution.py:393

commit v5 on v4

--- a/solution.py
+++ b/solution.py
@@ -80,6 +80,10 @@
         sent.append(cp)
         return cp
 
+    def drain():
+        while sent:
+            sent.pop(0).wait_send()
+
     a_cp = []
 
     def gather(h):
@@ -107,6 +111,9 @@
             Ahi[k * blk:(k + 1) * blk, cols] = hi
             Alo[k * blk:(k + 1) * blk, cols] = lo
 
+    drain()
+    gather(1)
+
     rh = blk // 2
     b_pc = ((0, 0, blk), (1, 0, rh), (1, rh, rh))
     d_pc = ((0, 0, rh), (0, rh, rh), (1, 0, blk))
@@ -163,9 +170,7 @@
             a_cp[h][i].wait_recv()
             fwd.append(send(G.at[h, p], G.at[h, p], a_s.at[h, 4 + i], a_r.at[h, 4 + i], (sib, z)))
         a_cp[h][3].wait_recv()
-        if h == 0:
-            gather(1)
-        else:
+        if h == 1:
             combine(0)
         for cp in fwd:
             cp.wait_recv()
@@ -224,7 +229,6 @@
             Bk[h, z, at:at + rh] = back[:, h * blk:(h + 1) * blk]
         d_send(n - 1)
         Ho[at:at + rh] = pre * sig
-    d_send(2)
     agg = jnp.concatenate([agg0, jnp.concatenate(agg1, axis=0)], axis=1)
     delta = jnp.concatenate(delta, axis=0)
     hid_cp = pltpu.make_async_copy(Ho, hid_o, loc_sem.at[5])
@@ -246,6 +250,14 @@
     g1 = send(wt.at[pl.ds(oth, half)], ws, g_s.at[0], g_r.at[0], (sib, z))
     relay(0)
     relay(1)
+    for n in (0, 1):
+        for i in range(3):
+            d_put(n, z, i, near).wait_send()
+    d_send(2)
+    drain()
+    for n in range(3):
+        for i in range(3):
+            b_put(n, z, i, near).wait_send()
     g1.wait_recv()
     wc[...] = wt[pl.ds(own, half)] + ws[...]
     g2 = [send(wc.at[pl.ds(pl.multiple_of((p // 2) * piece, piece), piece)], wr.at[i], g_s.at[1 + i], g_r.at[1 + i], (p, z))
@@ -331,12 +343,9 @@
     g6.wait_recv()
     g_cp = pltpu.make_async_copy(gw, gw_o, loc_sem.at[7])
     g_cp.start()
-    for cp in sent:
-        cp.wait_send()
-    for n in range(3):
-        for i in range(3):
-            b_put(n, z, i, near).wait_send()
-            d_put(n, z, i, near).wait_send()
+    drain()
+    for i in range(3):
+        d_put(2, z, i, near).wait_send()
     hid_cp.wait()
     f_cp.wait()
     g_cp.wait()

time: 49.4 us -> 51.5 us (1.043)
  Pallas kernels: 48.6 us -> 50.7 us
    pallas_call x1, Pallas kernels: 46.8 us -> 48.9 us  [fused(): pl.pallas_call(kernel, out_shape=(jax.ShapeDtypeStruct((blk, width), F32)...]
where the time goes in v5:
time: 51.5 us; the launch traced here: 51.4 us
  Pallas kernels  50.7 us (98%)
  between operations  0.64 us (1%)
    pallas_call x1, Pallas kernels, fused(): pl.pallas_call(kernel, out_shape=(jax.ShapeDtypeStruct((blk, width), F32)...  48.9 us
    pallas_call x1, Pallas kernels, fused(): pl.pallas_call(store, out_shape=tuple((jax.ShapeDtypeStruct(r.shape, r.dt...  1.81 us

profile of v5, /device:TPU:0, one launch (start us, length us, event | category | flops | bytes accessed | tf_op | source)
XLA Modules:
  0.0 51.4 jit_solution(5153554766638955672)
XLA Ops:
  0.6 48.9 %graph_step.1 = (f32[128,256]{1,0:T(8,128)}, f32[256,256]{1,0:T(8,128)}, f32[128,256]{1,0:T(8,128)}) custom-call(f32[128,256]{1,0:T(8,128)} %feat.1, f32[256,256]{1,0:T(8,128)} %weight.1, f32[128,256]{1,0:T(8,128)} %cot.1, f32[1,1,8,2,128,128]{5,4,3,2,1,0:T(8,128)} %tiles.1, s32[1,1,8]{2,1,0:T(1,128)} %cnt.1, s32[1,1,2,8]{3,2,1,0:T(2,128)} %bitcast.1), custom_call_target="tpu_custom_call" | custom-call | flops 1610612736 | bytes 1048576 | tf_op jit(solution)/shard_map/graph_step/pallas_call | solution.py:380
  49.5 1.8 %store_results.1 = (f32[128,256]{1,0:T(8,128)}, f32[256,256]{1,0:T(8,128)}, f32[128,256]{1,0:T(8,128)}) custom-call(f32[128,256]{1,0:T(8,128)} %get-tuple-element.6.a, f32[256,256]{1,0:T(8,128)} %get-tuple-element.7.b, f32[128,256]{1,0:T(8,128)} %get-tuple-element.8.c), custom_call_target="tpu_custom_call" | custom-call | tf_op jit(solution)/shard_map/store_results/pallas_call | solution.py:402

commit v6 on v5

--- a/solution.py
+++ b/solution.py
@@ -89,9 +89,10 @@
     def gather(h):
         loads[h].wait()
         mine = G.at[h, row]
-        a_cp.append([send(mine, mine, a_s.at[h, i], a_r.at[h, i], (p, z)) for i, p in enumerate((dg, xn, yn, sib))])
+        a_cp.append([send(mine, mine, a_s.at[h, i], a_r.at[h, i], (p, z)) for i, p in ((3, dg), (1, xn), (2, yn), (0, sib))])
 
     gather(0)
+    gather(1)
 
     loads[2].wait()
 
@@ -111,9 +112,6 @@
             Ahi[k * blk:(k + 1) * blk, cols] = hi
             Alo[k * blk:(k + 1) * blk, cols] = lo
 
-    drain()
-    gather(1)
-
     rh = blk // 2
     b_pc = ((0, 0, blk), (1, 0, rh), (1, rh, rh))
     d_pc = ((0, 0, rh), (0, rh, rh), (1, 0, blk))
@@ -164,21 +162,39 @@
         b_put(n, far, 1, far).wait_recv()
         return part + Rb[h, 1, at:at + size]
 
+    def pair_rhs(ref):
+        hi, lo = split(ref.reshape(2 * blk, blk))
+        return jnp.concatenate([hi, lo], axis=1)
+
+    def pair_mm(ah, al, rhs):
+        acc = mm(ah, rhs)
+        return acc[:, :blk] + (acc[:, blk:] + mm(al, rhs[:, :blk]))
+
+    def add_chip(h, chip, first=False):
+        cols = pl.ds(pl.multiple_of(chip * (2 * blk), 2 * blk), 2 * blk)
+        part = pair_mm(Ahi[:, cols], Alo[:, cols], pair_rhs(G[h, pl.ds(2 * chip, 2)])).reshape(reps, blk, blk)
+        Pb[h] = part if first else Pb[h] + part
+
     for h in range(2):
-        fwd = []
-        for i, p in ((1, xn), (2, yn), (0, dg)):
-            a_cp[h][i].wait_recv()
-            fwd.append(send(G.at[h, p], G.at[h, p], a_s.at[h, 4 + i], a_r.at[h, 4 + i], (sib, z)))
+
+        def forward(i, p):
+            put(G.at[h, p], G.at[h, p], a_s.at[h, i], a_r.at[h, i], (p, z)).wait_recv()
+            send(G.at[h, p], G.at[h, p], a_s.at[h, 3 + i], a_r.at[h, 3 + i], (sib, z))
+
+        forward(1, xn)
+        forward(2, yn)
         a_cp[h][3].wait_recv()
+        add_chip(h, q, True)
+        forward(3, dg)
         if h == 1:
             combine(0)
-        for cp in fwd:
-            cp.wait_recv()
-        fh, fl = split(G[h].reshape(secs * blk, blk))
-        rhs = jnp.concatenate([fh, fl], axis=1)
-        acc = mm(Ahi[...], rhs)
-        acc = acc[:, :blk] + (acc[:, blk:] + mm(Alo[...], fh))
-        Pb[h] = acc.reshape(reps, blk, blk)
+
+        @pl.loop(1, 4)
+        def _(i):
+            p = row + (i % 2) * (2 - 4 * x) + (i // 2) * (4 - 8 * y)
+            put(G.at[h, p], G.at[h, p], a_s.at[h, 3 + i], a_r.at[h, 3 + i], (sib, z)).wait_recv()
+            add_chip(h, p // 2)
+
         for n in ((0,), (1, 2))[h]:
             b_send(n)
 
@@ -229,6 +245,7 @@
             Bk[h, z, at:at + rh] = back[:, h * blk:(h + 1) * blk]
         d_send(n - 1)
         Ho[at:at + rh] = pre * sig
+    d_send(2)
     agg = jnp.concatenate([agg0, jnp.concatenate(agg1, axis=0)], axis=1)
     delta = jnp.concatenate(delta, axis=0)
     hid_cp = pltpu.make_async_copy(Ho, hid_o, loc_sem.at[5])
@@ -250,10 +267,6 @@
     g1 = send(wt.at[pl.ds(oth, half)], ws, g_s.at[0], g_r.at[0], (sib, z))
     relay(0)
     relay(1)
-    for n in (0, 1):
-        for i in range(3):
-            d_put(n, z, i, near).wait_send()
-    d_send(2)
     drain()
     for n in range(3):
         for i in range(3):
@@ -264,26 +277,34 @@
           for i, p in enumerate(plane)]
 
     def rows_start(h):
-        for n in ((0, 1), (2,))[h]:
+        parts = ((0, 1 - c), (1, c))
+        at = [pl.ds(pl.multiple_of(core * (chips * blk), chips * blk), chips * blk) for _, core in parts]
+
+        def pair(k):
+            cols = pl.ds(pl.multiple_of(k * blk, 2 * blk), 2 * blk)
+            rhs = pair_rhs(Bk[h, pl.ds(k, 2)])
+            return [lambda a=a: pair_mm(AThi[a, cols], ATlo[a, cols], rhs).reshape(chips, blk, blk) for a in at]
+
+        pieces = ((0, 1), (2,))[h]
+        for n in pieces:
             d_put(n, near, 0, near).wait_recv()
+        here = (z // 2) * 2
+        for i, part in enumerate(pair(here)):
+            Rs[h, i] = part()
+        for n in pieces:
             d_put(n, far, 1, far).wait_recv()
 
         @pl.when(outer)
         def _():
-            for n in ((0, 1), (2,))[h]:
+            for n in pieces:
                 d_put(n, mir, 2, mir).wait_recv()
 
-        bh, bl = split(Bk[h].reshape(quarter, blk))
-        rhs = jnp.concatenate([bh, bl], axis=1)
-        out = None
-        for first, core in ((True, 1 - c), (False, c)):
-            at = pl.ds(pl.multiple_of(core * (chips * blk), chips * blk), chips * blk)
-            acc = mm(AThi[at], rhs)
-            acc = acc[:, :blk] + (acc[:, blk:] + mm(ATlo[at], bh))
-            Rs[h, 0 if first else 1] = acc.reshape(chips, blk, blk)
-            if first:
-                out = [send(Rs.at[h, 0, p // 2], Es.at[h, p // 2], e_s.at[h, 3 + i], e_r.at[h, 3 + i], (sib, z))
-                       for i, p in enumerate((dg, xn, yn, row))]
+        out = []
+        for i, part in enumerate(pair(2 - here)):
+            Rs[h, i] = Rs[h, i] + part()
+            if i == 0:
+                out = [send(Rs.at[h, 0, p // 2], Es.at[h, p // 2], e_s.at[h, 3 + m], e_r.at[h, 3 + m], (sib, z))
+                       for m, p in enumerate((dg, xn, yn, row))]
         return out
 
     def rows_mid(h, cps):
@@ -344,8 +365,9 @@
     g_cp = pltpu.make_async_copy(gw, gw_o, loc_sem.at[7])
     g_cp.start()
     drain()
-    for i in range(3):
-        d_put(2, z, i, near).wait_send()
+    for n in range(3):
+        for i in range(3):
+            d_put(n, z, i, near).wait_send()
     hid_cp.wait()
     f_cp.wait()
     g_cp.wait()

time: 51.5 us -> 50.6 us (0.983)
  Pallas kernels: 50.7 us -> 49.8 us
    pallas_call x1, Pallas kernels: 48.9 us -> 48 us  [fused(): pl.pallas_call(kernel, out_shape=(jax.ShapeDtypeStruct((blk, width), F32)...]
where the time goes in v6:
time: 50.6 us; the launch traced here: 50.4 us
  Pallas kernels  49.8 us (98%)
  between operations  0.64 us (1%)
    pallas_call x1, Pallas kernels, fused(): pl.pallas_call(kernel, out_shape=(jax.ShapeDtypeStruct((blk, width), F32)...  48 us
    pallas_call x1, Pallas kernels, fused(): pl.pallas_call(store, out_shape=tuple((jax.ShapeDtypeStruct(r.shape, r.dt...  1.81 us

profile of v6, /device:TPU:0, one launch (start us, length us, event | category | flops | bytes accessed | tf_op | source)
XLA Modules:
  0.0 50.4 jit_solution(13878424765564722234)
XLA Ops:
  0.6 48.0 %graph_step.1 = (f32[128,256]{1,0:T(8,128)}, f32[256,256]{1,0:T(8,128)}, f32[128,256]{1,0:T(8,128)}) custom-call(f32[128,256]{1,0:T(8,128)} %feat.1, f32[256,256]{1,0:T(8,128)} %weight.1, f32[128,256]{1,0:T(8,128)} %cot.1, f32[1,1,8,2,128,128]{5,4,3,2,1,0:T(8,128)} %tiles.1, s32[1,1,8]{2,1,0:T(1,128)} %cnt.1, s32[1,1,2,8]{3,2,1,0:T(2,128)} %bitcast.1), custom_call_target="tpu_custom_call" | custom-call | flops 1610612736 | bytes 1048576 | tf_op jit(solution)/shard_map/graph_step/pallas_call | solution.py:402
  48.6 1.8 %store_results.1 = (f32[128,256]{1,0:T(8,128)}, f32[256,256]{1,0:T(8,128)}, f32[128,256]{1,0:T(8,128)}) custom-call(f32[128,256]{1,0:T(8,128)} %get-tuple-element.6.a, f32[256,256]{1,0:T(8,128)} %get-tuple-element.7.b, f32[128,256]{1,0:T(8,128)} %get-tuple-element.8.c), custom_call_target="tpu_custom_call" | custom-call | tf_op jit(solution)/shard_map/store_results/pallas_call | solution.py:424

commit v7 on v6

--- a/solution.py
+++ b/solution.py
@@ -92,7 +92,6 @@
         a_cp.append([send(mine, mine, a_s.at[h, i], a_r.at[h, i], (p, z)) for i, p in ((3, dg), (1, xn), (2, yn), (0, sib))])
 
     gather(0)
-    gather(1)
 
     loads[2].wait()
 
@@ -128,8 +127,6 @@
         @pl.when(outer)
         def _():
             stage_put(n).start()
-            b_put(n, far, 1, far).start()
-            b_put(n, near, 0, near).start()
 
         @pl.when(inner)
         def _():
@@ -145,20 +142,25 @@
             Pb[h, far, at:at + size] = Pb[h, far, at:at + size] + St[h, at:at + size]
             b_put(n, far, 1, far).start()
 
+        @pl.when(outer)
+        def _():
+            b_put(n, near, 0, near).wait_recv()
+            b_put(n, far, 1, far).start()
+            b_put(n, near, 0, near).start()
+
     def b_sum(n):
         h, at, size = b_pc[n]
-        b_put(n, near, 0, near).wait_recv()
-        part = Pb[h, z, at:at + size] + Rb[h, 0, at:at + size]
-
-        @pl.when(inner)
-        def _():
+
+        @pl.when(inner)
+        def _():
+            b_put(n, near, 0, near).wait_recv()
             b_put(n, mir, 2, mir).wait_recv()
 
         @pl.when(outer)
         def _():
             Rb[h, 2, at:at + size] = jnp.zeros((size, blk), F32)
 
-        part = part + Rb[h, 2, at:at + size]
+        part = Pb[h, z, at:at + size] + Rb[h, 0, at:at + size] + Rb[h, 2, at:at + size]
         b_put(n, far, 1, far).wait_recv()
         return part + Rb[h, 1, at:at + size]
 
@@ -186,7 +188,9 @@
         a_cp[h][3].wait_recv()
         add_chip(h, q, True)
         forward(3, dg)
-        if h == 1:
+        if h == 0:
+            gather(1)
+        else:
             combine(0)
 
         @pl.loop(1, 4)
@@ -222,11 +226,9 @@
         return put(ref, ref, d_s.at[n, slot], d_r.at[n, slot], (row, dev))
 
     def d_send(n):
-        d_put(n, z, 2, mir).start()
-
-        @pl.when(outer)
-        def _():
-            d_put(n, z, 1, far).start()
+        @pl.when(inner)
+        def _():
+            d_put(n, z, 2, mir).start()
 
         d_put(n, z, 0, near).start()
 
@@ -257,6 +259,12 @@
             d_put(n, mir, 2, mir).wait_recv()
             d_put(n, mir, 1, near).start()
 
+        @pl.when(outer)
+        def _():
+            d_put(n, near, 0, near).wait_recv()
+            d_put(n, z, 2, mir).start()
+            d_put(n, z, 1, far).start()
+
 
     wt[...] = mm3(agg.T, delta) * (1.0 / math.sqrt(blk * secs * reps))
     half = wt.shape[0] // 2
@@ -286,8 +294,12 @@
             return [lambda a=a: pair_mm(AThi[a, cols], ATlo[a, cols], rhs).reshape(chips, blk, blk) for a in at]
 
         pieces = ((0, 1), (2,))[h]
-        for n in pieces:
-            d_put(n, near, 0, near).wait_recv()
+
+        @pl.when(inner)
+        def _():
+            for n in pieces:
+                d_put(n, near, 0, near).wait_recv()
+
         here = (z // 2) * 2
         for i, part in enumerate(pair(here)):
             Rs[h, i] = part()
@@ -323,8 +335,8 @@
             total = total + Er[h, i]
         Fo[:, h * blk:(h + 1) * blk] = total
 
+    relay(2)
     e0 = rows_start(0)
-    relay(2)
     e0 = rows_mid(0, e0)
 
     at = pl.multiple_of(q * piece, piece)

time: 50.6 us -> 51.9 us (1.026)
  Pallas kernels: 49.8 us -> 51 us
    pallas_call x1, Pallas kernels: 48 us -> 49.2 us  [fused(): pl.pallas_call(kernel, out_shape=(jax.ShapeDtypeStruct((blk, width), F32)...]
where the time goes in v7:
time: 51.9 us; the launch traced here: 51.7 us
  Pallas kernels  51 us (98%)
  between operations  0.64 us (1%)
    pallas_call x1, Pallas kernels, fused(): pl.pallas_call(kernel, out_shape=(jax.ShapeDtypeStruct((blk, width), F32)...  49.2 us
    pallas_call x1, Pallas kernels, fused(): pl.pallas_call(store, out_shape=tuple((jax.ShapeDtypeStruct(r.shape, r.dt...  1.81 us

profile of v7, /device:TPU:0, one launch (start us, length us, event | category | flops | bytes accessed | tf_op | source)
XLA Modules:
  0.0 51.7 jit_solution(17381998889544196960)
XLA Ops:
  0.6 49.2 %graph_step.1 = (f32[128,256]{1,0:T(8,128)}, f32[256,256]{1,0:T(8,128)}, f32[128,256]{1,0:T(8,128)}) custom-call(f32[128,256]{1,0:T(8,128)} %feat.1, f32[256,256]{1,0:T(8,128)} %weight.1, f32[128,256]{1,0:T(8,128)} %cot.1, f32[1,1,8,2,128,128]{5,4,3,2,1,0:T(8,128)} %tiles.1, s32[1,1,8]{2,1,0:T(1,128)} %cnt.1, s32[1,1,2,8]{3,2,1,0:T(2,128)} %bitcast.1), custom_call_target="tpu_custom_call" | custom-call | flops 1610612736 | bytes 1048576 | tf_op jit(solution)/shard_map/graph_step/pallas_call | solution.py:414
  49.9 1.8 %store_results.1 = (f32[128,256]{1,0:T(8,128)}, f32[256,256]{1,0:T(8,128)}, f32[128,256]{1,0:T(8,128)}) custom-call(f32[128,256]{1,0:T(8,128)} %get-tuple-element.6.a, f32[256,256]{1,0:T(8,128)} %get-tuple-element.7.b, f32[128,256]{1,0:T(8,128)} %get-tuple-element.8.c), custom_call_target="tpu_custom_call" | custom-call | tf_op jit(solution)/shard_map/store_results/pallas_call | solution.py:436

commit v8 on v6

--- a/solution.py
+++ b/solution.py
@@ -92,7 +92,6 @@
         a_cp.append([send(mine, mine, a_s.at[h, i], a_r.at[h, i], (p, z)) for i, p in ((3, dg), (1, xn), (2, yn), (0, sib))])
 
     gather(0)
-    gather(1)
 
     loads[2].wait()
 
@@ -186,7 +185,9 @@
         a_cp[h][3].wait_recv()
         add_chip(h, q, True)
         forward(3, dg)
-        if h == 1:
+        if h == 0:
+            gather(1)
+        else:
             combine(0)
 
         @pl.loop(1, 4)

time: 50.6 us -> 49.2 us (0.972)
  Pallas kernels: 49.8 us -> 48.4 us
    pallas_call x1, Pallas kernels: 48 us -> 46.6 us  [fused(): pl.pallas_call(kernel, out_shape=(jax.ShapeDtypeStruct((blk, width), F32)...]
where the time goes in v8:
time: 49.2 us; the launch traced here: 49 us
  Pallas kernels  48.4 us (98%)
  between operations  0.64 us (1%)
    pallas_call x1, Pallas kernels, fused(): pl.pallas_call(kernel, out_shape=(jax.ShapeDtypeStruct((blk, width), F32)...  46.6 us
    pallas_call x1, Pallas kernels, fused(): pl.pallas_call(store, out_shape=tuple((jax.ShapeDtypeStruct(r.shape, r.dt...  1.81 us

profile of v8, /device:TPU:0, one launch (start us, length us, event | category | flops | bytes accessed | tf_op | source)
XLA Modules:
  0.0 49.0 jit_solution(195597061089869742)
XLA Ops:
  0.6 46.6 %graph_step.1 = (f32[128,256]{1,0:T(8,128)}, f32[256,256]{1,0:T(8,128)}, f32[128,256]{1,0:T(8,128)}) custom-call(f32[128,256]{1,0:T(8,128)} %feat.1, f32[256,256]{1,0:T(8,128)} %weight.1, f32[128,256]{1,0:T(8,128)} %cot.1, f32[1,1,8,2,128,128]{5,4,3,2,1,0:T(8,128)} %tiles.1, s32[1,1,8]{2,1,0:T(1,128)} %cnt.1, s32[1,1,2,8]{3,2,1,0:T(2,128)} %bitcast.1), custom_call_target="tpu_custom_call" | custom-call | flops 1610612736 | bytes 1048576 | tf_op jit(solution)/shard_map/graph_step/pallas_call | solution.py:403
  47.2 1.8 %store_results.1 = (f32[128,256]{1,0:T(8,128)}, f32[256,256]{1,0:T(8,128)}, f32[128,256]{1,0:T(8,128)}) custom-call(f32[128,256]{1,0:T(8,128)} %get-tuple-element.6.a, f32[256,256]{1,0:T(8,128)} %get-tuple-element.7.b, f32[128,256]{1,0:T(8,128)} %get-tuple-element.8.c), custom_call_target="tpu_custom_call" | custom-call | tf_op jit(solution)/shard_map/store_results/pallas_call | solution.py:425

commit v9 on v8

--- a/solution.py
+++ b/solution.py
@@ -246,7 +246,6 @@
             Bk[h, z, at:at + rh] = back[:, h * blk:(h + 1) * blk]
         d_send(n - 1)
         Ho[at:at + rh] = pre * sig
-    d_send(2)
     agg = jnp.concatenate([agg0, jnp.concatenate(agg1, axis=0)], axis=1)
     delta = jnp.concatenate(delta, axis=0)
     hid_cp = pltpu.make_async_copy(Ho, hid_o, loc_sem.at[5])
@@ -268,6 +267,13 @@
     g1 = send(wt.at[pl.ds(oth, half)], ws, g_s.at[0], g_r.at[0], (sib, z))
     relay(0)
     relay(1)
+
+    @pl.when(outer)
+    def _():
+        for n in (0, 1):
+            d_put(n, near, 0, near).wait_recv()
+
+    d_send(2)
     drain()
     for n in range(3):
         for i in range(3):
@@ -287,8 +293,14 @@
             return [lambda a=a: pair_mm(AThi[a, cols], ATlo[a, cols], rhs).reshape(chips, blk, blk) for a in at]
 
         pieces = ((0, 1), (2,))[h]
-        for n in pieces:
-            d_put(n, near, 0, near).wait_recv()
+        if h == 0:
+            @pl.when(inner)
+            def _():
+                for n in pieces:
+                    d_put(n, near, 0, near).wait_recv()
+        else:
+            for n in pieces:
+                d_put(n, near, 0, near).wait_recv()
         here = (z // 2) * 2
         for i, part in enumerate(pair(here)):
             Rs[h, i] = part()

time: 49.2 us -> 49.3 us (level)
  no operation moved by 1% of the time
where the time goes in v9:
time: 49.3 us; the launch traced here: 49.1 us
  Pallas kernels  48.5 us (98%)
  between operations  0.64 us (1%)
    pallas_call x1, Pallas kernels, fused(): pl.pallas_call(kernel, out_shape=(jax.ShapeDtypeStruct((blk, width), F32)...  46.7 us
    pallas_call x1, Pallas kernels, fused(): pl.pallas_call(store, out_shape=tuple((jax.ShapeDtypeStruct(r.shape, r.dt...  1.81 us

profile of v9, /device:TPU:0, one launch (start us, length us, event | category | flops | bytes accessed | tf_op | source)
XLA Modules:
  0.0 49.1 jit_solution(787981256507547889)
XLA Ops:
  0.6 46.7 %graph_step.1 = (f32[128,256]{1,0:T(8,128)}, f32[256,256]{1,0:T(8,128)}, f32[128,256]{1,0:T(8,128)}) custom-call(f32[128,256]{1,0:T(8,128)} %feat.1, f32[256,256]{1,0:T(8,128)} %weight.1, f32[128,256]{1,0:T(8,128)} %cot.1, f32[1,1,8,2,128,128]{5,4,3,2,1,0:T(8,128)} %tiles.1, s32[1,1,8]{2,1,0:T(1,128)} %cnt.1, s32[1,1,2,8]{3,2,1,0:T(2,128)} %bitcast.1), custom_call_target="tpu_custom_call" | custom-call | flops 1610612736 | bytes 1048576 | tf_op jit(solution)/shard_map/graph_step/pallas_call | solution.py:415
  47.3 1.8 %store_results.1 = (f32[128,256]{1,0:T(8,128)}, f32[256,256]{1,0:T(8,128)}, f32[128,256]{1,0:T(8,128)}) custom-call(f32[128,256]{1,0:T(8,128)} %get-tuple-element.6.a, f32[256,256]{1,0:T(8,128)} %get-tuple-element.7.b, f32[128,256]{1,0:T(8,128)} %get-tuple-element.8.c), custom_call_target="tpu_custom_call" | custom-call | tf_op jit(solution)/shard_map/store_results/pallas_call | solution.py:437
